TPU v7x, 128 devices: a whole 4x4x4 slice. The times are simulated.
128 devices in a mesh: dp: 4 (over x), ctx: 32 (over z, y, core).
Axes of the slice: x: 4, y: 4, z: 4, core: 2. Of those that a mesh axis runs over, the one named last changes fastest.
Arguments:
- inputs: bfloat16 [16384, 896], P(('dp', 'ctx')), may hold values from -6 to 6
- cotangent: bfloat16 [16384, 896], P(('dp', 'ctx')), may hold values from -6 to 6
- span_order: int32 [64], replicated, may hold values from 0 to 63, as said below
- positions: int32 [16384], P(('dp', 'ctx')), may hold values from 0 to 1023, as said below
- attn_gain: bfloat16 [896], P('dp'), may hold values from 0.5 to 1.5
- qkv_weight: bfloat16 [896, 1152], P('dp'), may hold values from -0.1875 to 0.1875
- qkv_bias: bfloat16 [1152], P('dp'), may hold values from -3 to 3
- out_weight: bfloat16 [896, 896], P('dp'), may hold values from -0.375 to 0.375
- mlp_gain: bfloat16 [896], P('dp'), may hold values from 0.5 to 1.5
- gate_weight: bfloat16 [896, 4864], P('dp'), may hold values from -0.1875 to 0.1875
- up_weight: bfloat16 [896, 4864], P('dp'), may hold values from -0.1875 to 0.1875
- down_weight: bfloat16 [4864, 896], P('dp'), may hold values from -0.078125 to 0.078125
Outputs:
- output: bfloat16 [16384, 896], P(('dp', 'ctx'))
- input_grad: bfloat16 [16384, 896], P(('dp', 'ctx'))
- attn_gain_grad: float32 [896], P('dp')
- qkv_weight_grad: float32 [896, 1152], P('dp')
- qkv_bias_grad: float32 [1024], P('dp')
- value_bias_grad: float32 [128], P('dp')
- out_weight_grad: float32 [896, 896], P('dp')
- mlp_gain_grad: float32 [896], P('dp')
- gate_weight_grad: float32 [896, 4864], P('dp')
- up_weight_grad: float32 [896, 4864], P('dp')
- down_weight_grad: float32 [4864, 896], P('dp')
Inputs may be any that keep to these rules, and one draw needn't show every extreme that they name: `span_order`: entries 2c and 2c + 1 hold two spans j and 63 - j, in either order; every span appears once. `positions`: each token's position within its document. Documents are runs of consecutive places of a sequence, none longer than 1024 tokens, and positions count from 0 at a run's start, increasing by one along place.
All inputs are finite; a program needn't handle non-finite values.
Results may differ from a plain program's by a relative error of at most 0.03.
Values may be sent and summed in bfloat16 or wider, within the bound.
A program may use at most 192 MiB of HBM per device.

v0:
```python
import jax
import jax.numpy as jnp
from jax import lax
from jax.sharding import PartitionSpec as P

QH = 14
KVH = 2
HD = 64
norm_eps = 1e-06
rope_base = 1000000.0
masked_score = -1e30


def rms_apply(values, gain):
    mean_square = jnp.mean(values * values, axis=-1, keepdims=True)
    return values * lax.rsqrt(mean_square + norm_eps) * gain


def half_turn(values):
    middle = values.shape[-1] // 2
    return jnp.concatenate([-values[..., middle:], values[..., :middle]], axis=-1)


def rotate(values, cosine, sine):
    return values * cosine + half_turn(values) * sine


def rope_tables(positions, head_dim):
    middle = head_dim // 2
    inverse = rope_base ** (-(jnp.arange(middle).astype(jnp.float32) * 2.0) / head_dim)
    angles = positions.astype(jnp.float32)[:, None] * inverse[None, :]
    angles = jnp.concatenate([angles, angles], axis=-1)
    return (jnp.cos(angles), jnp.sin(angles))


def span_lookup(table, slots):
    picked = slots[:, None] == jnp.arange(table.shape[0], dtype=jnp.int32)[None, :]
    return jnp.sum(jnp.where(picked, table[None, :], 0), axis=1)


def swiglu(gate_in, up_in):
    return jax.nn.silu(gate_in) * up_in


def body(
    inputs,
    cotangent,
    span_order,
    positions,
    attn_gain,
    qkv_weight,
    qkv_bias,
    out_weight,
    mlp_gain,
    gate_weight,
    up_weight,
    down_weight,
):
    token_count = inputs.shape[0]
    span_rows = token_count // 2
    head_dim = HD
    query_heads = QH
    kv_heads = KVH
    group_size = query_heads // kv_heads
    score_scale = head_dim ** (-0.5)
    q_cols = query_heads * head_dim
    k_cols = kv_heads * head_dim
    seq_length = token_count * lax.axis_size("ctx")
    key_block = min(1024, seq_length)
    block_count = seq_length // key_block
    device_slot = lax.axis_index("ctx")
    local_slots = jnp.arange(token_count, dtype=jnp.int32)
    query_places = (
        span_lookup(span_order, 2 * device_slot + local_slots // span_rows) * span_rows
        + local_slots % span_rows
    )
    all_slots = jnp.arange(seq_length, dtype=jnp.int32)
    key_places = span_lookup(span_order, all_slots // span_rows) * span_rows + all_slots % span_rows
    key_places = key_places.reshape(block_count, key_block)
    gain_one, qkv_full, bias_full, out_full = (
        lax.all_gather(attn_gain, "dp", axis=0, tiled=True),
        lax.all_gather(qkv_weight, "dp", axis=0, tiled=True),
        lax.all_gather(qkv_bias, "dp", axis=0, tiled=True),
        lax.all_gather(out_weight, "dp", axis=0, tiled=True),
    )
    inputs_wide = inputs.astype(jnp.float32)
    gain_one_wide = gain_one.astype(jnp.float32)
    normed_one = rms_apply(inputs_wide, gain_one_wide).astype(jnp.bfloat16)
    mixed_proj = jnp.dot(
        normed_one, qkv_full, preferred_element_type=jnp.float32
    ) + bias_full.astype(jnp.float32)
    cosine, sine = rope_tables(positions, head_dim)
    cosine = cosine[:, None, :]
    sine = sine[:, None, :]
    query_rot = rotate(
        mixed_proj[:, :q_cols].reshape(token_count, query_heads, head_dim), cosine, sine
    ).astype(jnp.bfloat16)
    key_rot = rotate(
        mixed_proj[:, q_cols : q_cols + k_cols].reshape(token_count, kv_heads, head_dim),
        cosine,
        sine,
    )
    key_rot = key_rot.astype(jnp.bfloat16).reshape(token_count, k_cols)
    value_low = mixed_proj[:, q_cols + k_cols :].astype(jnp.bfloat16)
    key_all, value_all = (
        lax.all_gather(key_rot, "ctx", axis=0, tiled=True),
        lax.all_gather(value_low, "ctx", axis=0, tiled=True),
    )
    key_blocks = key_all.reshape(block_count, key_block, kv_heads, head_dim)
    value_blocks = value_all.reshape(block_count, key_block, kv_heads, head_dim)
    query_grouped = query_rot.reshape(token_count, kv_heads, group_size, head_dim)

    def block_scores(key_part, place_part):
        scores = (
            jnp.einsum(
                "qhgd,khd->hgqk", query_grouped, key_part, preferred_element_type=jnp.float32
            )
            * score_scale
        )
        allowed = place_part[None, :] <= query_places[:, None]
        return jnp.where(allowed[None, None], scores, masked_score)

    def max_step(running, pieces):
        running_max, running_sum = running
        scores = block_scores(pieces[0], pieces[1])
        new_max = jnp.maximum(running_max, jnp.max(scores, axis=-1))
        new_sum = running_sum * jnp.exp(running_max - new_max) + jnp.sum(
            jnp.exp(scores - new_max[..., None]), axis=-1
        )
        return ((new_max, new_sum), None)

    start_max = jnp.full((kv_heads, group_size, token_count), masked_score, jnp.float32)
    start_sum = jnp.zeros((kv_heads, group_size, token_count), jnp.float32)
    (final_max, final_sum), unused = lax.scan(
        max_step, (start_max, start_sum), (key_blocks, key_places)
    )
    log_total = final_max + jnp.log(final_sum)

    def value_step(attended_sum, pieces):
        scores = block_scores(pieces[0], pieces[2])
        probs_low = jnp.exp(scores - log_total[..., None]).astype(jnp.bfloat16)
        return (
            attended_sum
            + jnp.einsum(
                "hgqk,khd->qhgd", probs_low, pieces[1], preferred_element_type=jnp.float32
            ),
            None,
        )

    start_total = jnp.zeros((token_count, kv_heads, group_size, head_dim), jnp.float32)
    attended_sum, unused = lax.scan(value_step, start_total, (key_blocks, value_blocks, key_places))
    attended_low = attended_sum.reshape(token_count, q_cols).astype(jnp.bfloat16)
    residual = inputs_wide + jnp.dot(attended_low, out_full, preferred_element_type=jnp.float32)
    gain_two, gate_full, up_full, down_full = (
        lax.all_gather(mlp_gain, "dp", axis=0, tiled=True),
        lax.all_gather(gate_weight, "dp", axis=0, tiled=True),
        lax.all_gather(up_weight, "dp", axis=0, tiled=True),
        lax.all_gather(down_weight, "dp", axis=0, tiled=True),
    )
    gain_two_wide = gain_two.astype(jnp.float32)
    normed_two = rms_apply(residual, gain_two_wide).astype(jnp.bfloat16)
    gate_proj = jnp.dot(normed_two, gate_full, preferred_element_type=jnp.float32)
    up_proj = jnp.dot(normed_two, up_full, preferred_element_type=jnp.float32)
    hidden_low = swiglu(gate_proj, up_proj).astype(jnp.bfloat16)
    output = (residual + jnp.dot(hidden_low, down_full, preferred_element_type=jnp.float32)).astype(
        jnp.bfloat16
    )
    d_hidden = jnp.dot(cotangent, down_full.T, preferred_element_type=jnp.float32)
    down_grad = jnp.dot(hidden_low.T, cotangent, preferred_element_type=jnp.float32)
    swiglu_back = jax.vjp(swiglu, gate_proj, up_proj)[1]
    d_gate, d_up = swiglu_back(d_hidden)
    d_gate = d_gate.astype(jnp.bfloat16)
    d_up = d_up.astype(jnp.bfloat16)
    gate_grad = jnp.dot(normed_two.T, d_gate, preferred_element_type=jnp.float32)
    up_grad = jnp.dot(normed_two.T, d_up, preferred_element_type=jnp.float32)
    d_normed_two = jnp.dot(d_gate, gate_full.T, preferred_element_type=jnp.float32) + jnp.dot(
        d_up, up_full.T, preferred_element_type=jnp.float32
    )
    norm_two_back = jax.vjp(rms_apply, residual, gain_two_wide)[1]
    d_resid_part, gain_two_grad = norm_two_back(d_normed_two)
    d_residual = d_resid_part + cotangent.astype(jnp.float32)
    d_branch = d_residual.astype(jnp.bfloat16)
    out_grad = jnp.dot(attended_low.T, d_branch, preferred_element_type=jnp.float32)
    d_attended = jnp.dot(d_branch, out_full.T, preferred_element_type=jnp.float32).astype(
        jnp.bfloat16
    )
    d_attended = d_attended.reshape(token_count, kv_heads, group_size, head_dim)
    row_delta = jnp.einsum("qhgd,qhgd->hgq", d_attended.astype(jnp.float32), attended_sum)

    def grad_step(d_query, pieces):
        key_part, value_part, place_part = pieces
        scores = block_scores(key_part, place_part)
        probs_full = jnp.exp(scores - log_total[..., None])
        probs_low = probs_full.astype(jnp.bfloat16)
        d_probs = jnp.einsum(
            "qhgd,khd->hgqk", d_attended, value_part, preferred_element_type=jnp.float32
        )
        d_scores = (probs_full * (d_probs - row_delta[..., None])).astype(jnp.bfloat16)
        d_query = (
            d_query
            + jnp.einsum("hgqk,khd->qhgd", d_scores, key_part, preferred_element_type=jnp.float32)
            * score_scale
        )
        d_key = (
            jnp.einsum(
                "hgqk,qhgd->khd", d_scores, query_grouped, preferred_element_type=jnp.float32
            )
            * score_scale
        )
        d_value = jnp.einsum(
            "hgqk,qhgd->khd", probs_low, d_attended, preferred_element_type=jnp.float32
        )
        return (d_query, (d_key, d_value))

    d_query, (d_key_blocks, d_value_blocks) = lax.scan(
        grad_step, start_total, (key_blocks, value_blocks, key_places)
    )
    d_key_all = d_key_blocks.reshape(seq_length, k_cols)
    d_value_all = d_value_blocks.reshape(seq_length, k_cols)
    d_key_own, d_value_own = (
        lax.psum_scatter(
            d_key_all.astype(jnp.bfloat16), "ctx", scatter_dimension=0, tiled=True
        ).astype(jnp.float32),
        lax.psum_scatter(
            d_value_all.astype(jnp.bfloat16), "ctx", scatter_dimension=0, tiled=True
        ).astype(jnp.float32),
    )

    def turn_back(grads):
        return jax.vjp(lambda values: rotate(values, cosine, sine), grads)[1](grads)[0]

    d_query_raw = turn_back(d_query.reshape(token_count, query_heads, head_dim)).reshape(
        token_count, q_cols
    )
    d_key_raw = turn_back(d_key_own.reshape(token_count, kv_heads, head_dim)).reshape(
        token_count, k_cols
    )
    d_mixed = jnp.concatenate([d_query_raw, d_key_raw, d_value_own], axis=1).astype(jnp.bfloat16)
    qkv_grad = jnp.dot(normed_one.T, d_mixed, preferred_element_type=jnp.float32)
    bias_grad = jnp.sum(d_mixed.astype(jnp.float32), axis=0)
    qk_bias_grad = bias_grad[: q_cols + k_cols]
    value_bias_grad = bias_grad[q_cols + k_cols :]
    d_normed_one = jnp.dot(d_mixed, qkv_full.T, preferred_element_type=jnp.float32)
    norm_one_back = jax.vjp(rms_apply, inputs_wide, gain_one_wide)[1]
    d_input_part, gain_one_grad = norm_one_back(d_normed_one)
    input_grad = (d_input_part + d_residual).astype(jnp.bfloat16)
    local_grads = (
        gain_one_grad,
        qkv_grad,
        qk_bias_grad,
        value_bias_grad,
        out_grad,
        gain_two_grad,
        gate_grad,
        up_grad,
        down_grad,
    )
    shard_grads = (
        lax.psum_scatter(
            local_grads[0].astype(jnp.bfloat16), "dp", scatter_dimension=0, tiled=True
        ).astype(jnp.float32),
        lax.psum_scatter(
            local_grads[1].astype(jnp.bfloat16), "dp", scatter_dimension=0, tiled=True
        ).astype(jnp.float32),
        lax.psum_scatter(
            local_grads[2].astype(jnp.bfloat16), "dp", scatter_dimension=0, tiled=True
        ).astype(jnp.float32),
        lax.psum_scatter(
            local_grads[3].astype(jnp.bfloat16), "dp", scatter_dimension=0, tiled=True
        ).astype(jnp.float32),
        lax.psum_scatter(
            local_grads[4].astype(jnp.bfloat16), "dp", scatter_dimension=0, tiled=True
        ).astype(jnp.float32),
        lax.psum_scatter(
            local_grads[5].astype(jnp.bfloat16), "dp", scatter_dimension=0, tiled=True
        ).astype(jnp.float32),
        lax.psum_scatter(
            local_grads[6].astype(jnp.bfloat16), "dp", scatter_dimension=0, tiled=True
        ).astype(jnp.float32),
        lax.psum_scatter(
            local_grads[7].astype(jnp.bfloat16), "dp", scatter_dimension=0, tiled=True
        ).astype(jnp.float32),
        lax.psum_scatter(
            local_grads[8].astype(jnp.bfloat16), "dp", scatter_dimension=0, tiled=True
        ).astype(jnp.float32),
    )
    summed = (
        lax.psum(shard_grads[0].astype(jnp.bfloat16), "ctx").astype(jnp.float32),
        lax.psum(shard_grads[1].astype(jnp.bfloat16), "ctx").astype(jnp.float32),
        lax.psum(shard_grads[2].astype(jnp.bfloat16), "ctx").astype(jnp.float32),
        lax.psum(shard_grads[3].astype(jnp.bfloat16), "ctx").astype(jnp.float32),
        lax.psum(shard_grads[4].astype(jnp.bfloat16), "ctx").astype(jnp.float32),
        lax.psum(shard_grads[5].astype(jnp.bfloat16), "ctx").astype(jnp.float32),
        lax.psum(shard_grads[6].astype(jnp.bfloat16), "ctx").astype(jnp.float32),
        lax.psum(shard_grads[7].astype(jnp.bfloat16), "ctx").astype(jnp.float32),
        lax.psum(shard_grads[8].astype(jnp.bfloat16), "ctx").astype(jnp.float32),
    )
    return (
        output,
        input_grad,
        summed[0],
        summed[1],
        summed[2],
        summed[3],
        summed[4],
        summed[5],
        summed[6],
        summed[7],
        summed[8],
    )


def solution(mesh):
    placed = (
        P(("dp", "ctx"), None),
        P(("dp", "ctx"), None),
        P(),
        P(("dp", "ctx")),
        P("dp"),
        P("dp", None),
        P("dp"),
        P("dp", None),
        P("dp"),
        P("dp", None),
        P("dp", None),
        P("dp", None),
    )
    return jax.shard_map(
        body,
        mesh=mesh,
        in_specs=placed,
        out_specs=(
            P(("dp", "ctx"), None),
            P(("dp", "ctx"), None),
            P("dp"),
            P("dp", None),
            P("dp"),
            P("dp"),
            P("dp", None),
            P("dp"),
            P("dp", None),
            P("dp", None),
            P("dp", None),
        ),
        check_vma=False,
    )
```

profile of v0, /device:TPU:1, one launch (start us, length us, event | category | flops | bytes accessed | tf_op | source)
XLA Modules:
  0.0 1149.0 jit_solution(3470323007845369848)
XLA Ops:
  13.2 9.4 all-reduce.14
  23.7 19.9 %all-gather.8.cloned.1.call-done = bf16[896,1152]{1,0:T(8,128)(2,1)} async-done(((bf16[224,1152]{1,0:T(8,128)(2,1)}), bf16[896,1152]{1,0:T(8,128)(2,1)}) %all-gather.8.cloned.1.call-update) | async-done | bytes 2064400 | tf_op jit(solution)/shard_map/all_gather | solution.py:82
  51.1 38.8 %all-gather.10.cloned.1.call-done = bf16[4096,128]{1,0:T(8,128)(2,1)} async-done(((bf16[128,128]{1,0:T(8,128)(2,1)}), bf16[4096,128]{1,0:T(8,128)(2,1)}) %all-gather.10.cloned.1.call-update) | async-done | bytes 1048592 | tf_op jit(solution)/shard_map/all_gather | solution.py:107
  89.9 5.0 reshape.338
  94.9 5.9 copy.88
  100.7 34.2 %all-gather.12.cloned.1.call-done = bf16[4096,128]{1,0:T(8,128)(2,1)} async-done(((bf16[128,128]{1,0:T(8,128)(2,1)}), bf16[4096,128]{1,0:T(8,128)(2,1)}) %all-gather.12.cloned.1.call-update) | async-done | bytes 1048592 | tf_op jit(solution)/shard_map/all_gather | solution.py:106
  134.9 5.0 reshape.339
  139.9 4.6 copy.89
  144.5 37.0 %while.39 = (s32[]{:T(128)}, f32[2,7,128]{2,1,0:T(8,128)S(1)}, f32[2,7,128]{2,1,0:T(8,128)S(1)}, s32[4,1024]{1,0:T(4,128)S(1)}, s32[128]{0:T(128)S(1)}, /*index=...) while((s32[]{:T(128)}, f32[2,7,128]{2,1,0:T(8,128)S(1)}, ...), condition=%wide.region_6.7_spmd.clone, body=%wide.region_3.6_spmd.clone.sunk | while | flops 247866112 | bytes 15670904 | solution.py:134
  148.9 4.6 exponential_reduce_fusion.2
  157.9 4.6 exponential_reduce_fusion.2
  171.7 4.7 fusion.161
  176.3 5.2 exponential_reduce_fusion.2
  181.6 15.2 %while.40 = (s32[]{:T(128)}, f32[128,2,7,64]{0,3,2,1:T(8,128)S(1)}, bf16[4,1024,2,64]{1,3,2,0:T(8,128)(2,1)}, s32[4,1024]{1,0:T(4,128)S(1)}, s32[128]{0:T(128)S(...) while((s32[]{:T(128)}, f32[128,2,7,64]{0,3,2,1:T(8,128)S(1)}, ...), condition=%wide.region_8.9_spmd.clone, body=%wide.region_7.8_spmd.clone.sunk | while | flops 477462528 | bytes 1955962 | solution.py:151
  199.9 49.5 %all-gather.16.cloned.1.call-done = bf16[896,4864]{1,0:T(8,128)(2,1)} async-done(((bf16[224,4864]{1,0:T(8,128)(2,1)}), bf16[896,4864]{1,0:T(8,128)(2,1)}) %all-gather.16.cloned.1.call-update) | async-done | bytes 8716304 | tf_op jit(solution)/shard_map/all_gather | solution.py:156
  249.4 6.4 fusion.102
  255.8 81.9 %all-gather.18.cloned.1.call-done = bf16[896,4864]{1,0:T(8,128)(2,1)} async-done(((bf16[224,4864]{1,0:T(8,128)(2,1)}), bf16[896,4864]{1,0:T(8,128)(2,1)}) %all-gather.18.cloned.1.call-update) | async-done | bytes 8716304 | tf_op jit(solution)/shard_map/all_gather | solution.py:157
  337.7 6.4 fusion.103
  344.1 82.1 %all-gather.20.cloned.1.call-done = bf16[4864,896]{1,0:T(8,128)(2,1)} async-done(((bf16[1216,896]{1,0:T(8,128)(2,1)}), bf16[4864,896]{1,0:T(8,128)(2,1)}) %all-gather.20.cloned.1.call-update) | async-done | bytes 8716304 | tf_op jit(solution)/shard_map/all_gather | solution.py:158
  426.3 7.5 multiply_convert_fusion
  433.8 7.2 fusion.104
  449.2 71.3 %while.41 = (s32[]{:T(128)}, f32[128,2,7,64]{0,3,2,1:T(8,128)S(1)}, bf16[4,1024,2,64]{1,3,2,0:T(8,128)(2,1)}, bf16[4,1024,2,64]{1,3,2,0:T(8,128)(2,1)}, bf16[4,1...) while((s32[]{:T(128)}, f32[128,2,7,64]{0,3,2,1:T(8,128)S(1)}, ...), condition=%wide.region_12.13_spmd.clone, body=%wide.region_11.12_spmd.clone.sunk | while | flops 1193361408 | bytes 99781520 | solution.py:215
  450.8 5.4 fusion.179
  460.9 5.2 fusion.182
  468.6 5.4 fusion.179
  478.7 5.2 fusion.182
  486.4 5.4 fusion.179
  496.5 5.2 fusion.182
  504.1 5.4 fusion.179
  514.3 5.2 fusion.182
  520.5 6.0 copy.124
  526.5 4.7 reshape.332
  531.3 6.0 copy.123
  537.3 4.7 reshape.330
  544.2 64.3 %reduce-scatter.24.cloned.1.call-done = bf16[128,128]{1,0:T(8,128)(2,1)} async-done(((bf16[4096,128]{1,0:T(8,128)(2,1)}), bf16[128,128]{1,0:T(8,128)(2,1)}) %reduce-scatter.24.cloned.1.call-update) | async-done | bytes 32784
  609.3 80.0 %reduce-scatter.22.cloned.1.call-done = bf16[128,128]{1,0:T(8,128)(2,1)} async-done(((bf16[4096,128]{1,0:T(8,128)(2,1)}), bf16[128,128]{1,0:T(8,128)(2,1)}) %reduce-scatter.22.cloned.1.call-update) | async-done | bytes 32784
  692.7 7.2 convolution_convert_fusion.2
  699.9 7.2 convolution_convert_fusion.1
  708.0 4.7 convolution_convert_fusion
  712.9 5.3 reduce-scatter.14.cloned.1.call-done
  718.2 32.8 %reduce-scatter.12.cloned.1.call-done = bf16[224,1152]{1,0:T(8,128)(2,1)} async-done(((bf16[896,1152]{1,0:T(8,128)(2,1)}), bf16[224,1152]{1,0:T(8,128)(2,1)}) %reduce-scatter.12.cloned.1.call-update) | async-done | bytes 516112 | tf_op jit(solution)/shard_map/reduce_scatter | solution.py:262
  751.0 85.4 %reduce-scatter.16.cloned.1.call-done = bf16[224,4864]{1,0:T(8,128)(2,1)} async-done(((bf16[896,4864]{1,0:T(8,128)(2,1)}), bf16[224,4864]{1,0:T(8,128)(2,1)}) %reduce-scatter.16.cloned.1.call-update) | async-done | bytes 2179088 | tf_op jit(solution)/shard_map/reduce_scatter | solution.py:277
  836.4 85.4 %reduce-scatter.18.cloned.1.call-done = bf16[224,4864]{1,0:T(8,128)(2,1)} async-done(((bf16[896,4864]{1,0:T(8,128)(2,1)}), bf16[224,4864]{1,0:T(8,128)(2,1)}) %reduce-scatter.18.cloned.1.call-update) | async-done | bytes 2179088 | tf_op jit(solution)/shard_map/reduce_scatter | solution.py:280
  921.7 85.4 %reduce-scatter.20.cloned.1.call-done = bf16[1216,896]{1,0:T(8,128)(2,1)} async-done(((bf16[4864,896]{1,0:T(8,128)(2,1)}), bf16[1216,896]{1,0:T(8,128)(2,1)}) %reduce-scatter.20.cloned.1.call-update) | async-done | bytes 2179088 | tf_op jit(solution)/shard_map/reduce_scatter | solution.py:283
  1009.2 5.8 fusion.65
  1016.0 7.1 all-reduce.13
  1023.4 65.2 %all-reduce.11 = (bf16[224]{0:T(256)(128)(2,1)S(1)}, bf16[256]{0:T(256)(128)(2,1)S(1)}, bf16[32]{0:T(256)(128)(2,1)S(1)}, bf16[224]{0:T(256)(128)(2,1)S(1)}) all-reduce(bf16[224]{0:T(256)(128)(2,1)S(1)} %dynamic-slice.4, bf16[256]{0:T(256)(128)(2,1)S(1)} %dynamic-slice.6, ...), channel_id=1, replica_groups=mesh['dp'=4,'ctx'=32] {'ctx'}, use_global_device_ids=true, to_apply=%region_18.19 | all-reduce | flops 736 | bytes 2944 | tf_op jit(solution)/shard_map/psum | solution.py:288
  1091.7 39.1 %all-reduce.17.cloned.1.call-done = (bf16[224,1152]{1,0:T(8,128)(2,1)}, bf16[224,896]{1,0:T(8,128)(2,1)}, bf16[224,4864]{1,0:T(8,128)(2,1)}, bf16[224,4864]{1,0:T(8,128)(2,1)}, bf16[1216,896]{1,0:T(8,128)(2,1)}) async-done(((bf16[224,1152]{1,0:T(8,128)(2,1)}, bf16[224,896]{1,0:T(8,128)(2,1)}, bf16[224,4864]{1,0:T(8,128)(2,1)}, bf16[224,4864]{1,0:T(8,128)(2,1)}, bf16[1216,896]{1,0:T(8,128)(2,1)}), ...) | async-done | bytes 7454736 | tf_op jit(solution)/shard_map/psum | solution.py:289
  (283 shorter events, 107.9 us)
Async XLA Ops:
  7.2 39.3 %copy-start.31 = (s32[128]{0:T(128)S(1)}, s32[128]{0:T(128)}, u32[]{:S(2)}) copy-start(s32[128]{0:T(128)} %param.21) | copy-start | bytes 1540
  7.2 36.4 %all-gather.8.cloned.1.call-start = ((), (), s32[]{:S(2)}) async-start(), calls=%async_computation.7 | async-start | bytes 2580480 | tf_op jit(solution)/shard_map/all_gather | solution.py:82
  7.9 82.0 %all-gather.10.cloned.1.call-start = ((), (), s32[]{:S(2)}) async-start(), calls=%async_computation.8 | async-start | bytes 1081344 | tf_op jit(solution)/shard_map/all_gather | solution.py:107
  23.7 23.3 %copy-start.29 = (f32[128]{0:T(128)}, f32[128]{0:T(128)S(1)}, u32[]{:S(2)}) copy-start(f32[128]{0:T(128)S(1)} %fusion.73) | copy-start | bytes 1540
  46.5 88.4 %all-gather.12.cloned.1.call-start = ((), (), s32[]{:S(2)}) async-start(), calls=%async_computation.9 | async-start | bytes 1081344 | tf_op jit(solution)/shard_map/all_gather | solution.py:106
  47.7 149.1 %all-gather.14.cloned.1.call-start = ((), (), s32[]{:S(2)}) async-start(), calls=%async_computation.10 | async-start | bytes 2007040 | tf_op jit(solution)/shard_map/all_gather | solution.py:84
  48.3 201.1 %all-gather.16.cloned.1.call-start = ((), (), s32[]{:S(2)}) async-start(), calls=%async_computation.11 | async-start | bytes 10895360 | tf_op jit(solution)/shard_map/all_gather | solution.py:156
  48.9 288.8 %all-gather.18.cloned.1.call-start = ((), (), s32[]{:S(2)}) async-start(), calls=%async_computation.12 | async-start | bytes 10895360 | tf_op jit(solution)/shard_map/all_gather | solution.py:157
  49.5 376.8 %all-gather.20.cloned.1.call-start = ((), (), s32[]{:S(2)}) async-start(), calls=%async_computation.13 | async-start | bytes 10895360 | tf_op jit(solution)/shard_map/all_gather | solution.py:158
  50.2 558.2 %reduce-scatter.24.cloned.1.call-start = ((), (), s32[]{:S(2)}) async-start(), calls=%async_computation.20 | async-start | bytes 1081344
  181.5 15.3 %copy-start.9 = (bf16[128,896]{1,0:T(8,128)(2,1)S(1)}, bf16[128,896]{1,0:T(8,128)(2,1)}, u32[]{:S(2)}) copy-start(bf16[128,896]{1,0:T(8,128)(2,1)} %param.18) | copy-start | bytes 688132
  196.7 59.0 %copy-start.19 = (f32[128,2,7,64]{0,3,2,1:T(8,128)}, f32[128,2,7,64]{0,3,2,1:T(8,128)S(1)}, u32[]{:S(2)}) copy-start(f32[128,2,7,64]{0,3,2,1:T(8,128)S(1)} %get-tuple-element.157) | copy-start | bytes 1376260
  196.8 59.0 %copy-start.17 = (bf16[128,2,7,64]{0,3,2,1:T(8,128)(2,1)}, bf16[128,2,7,64]{0,3,2,1:T(8,128)(2,1)S(1)}, u32[]{:S(2)}) copy-start(bf16[128,2,7,64]{0,3,2,1:T(8,128)(2,1)S(1)} %convert_element_type.171) | copy-start | bytes 688132
  433.8 7.2 copy-start.12
  433.8 7.2 copy-start.11
  433.8 7.2 copy-start.2
  433.8 7.2 copy-start.4
  441.1 3.9 copy-start.8
  450.5 5.7 copy-start.1
  456.2 4.7 copy-start.22
  456.2 4.7 copy-start.27
  460.9 5.3 copy-start.21
  468.3 5.7 copy-start.1
  474.0 4.7 copy-start.22
  474.0 4.7 copy-start.27
  478.7 5.3 copy-start.21
  486.1 5.7 copy-start.1
  491.8 4.7 copy-start.22
  491.8 4.7 copy-start.27
  496.4 5.3 copy-start.21
  503.9 5.7 copy-start.1
  509.6 4.7 copy-start.22
  509.6 4.7 copy-start.27
  514.2 5.3 copy-start.21
  531.2 158.1 %reduce-scatter.22.cloned.1.call-start = ((), (), s32[]{:S(2)}) async-start(), calls=%async_computation.19 | async-start | bytes 1081344
  531.3 10.9 copy-start.7
  531.3 10.9 copy-start.18
  542.1 148.1 %copy-start.10 = (bf16[128,896]{1,0:T(8,128)(2,1)S(1)}, bf16[128,896]{1,0:T(8,128)(2,1)}, u32[]{:S(2)}) copy-start(bf16[128,896]{1,0:T(8,128)(2,1)} %param.18) | copy-start | bytes 688132
  542.1 176.0 %reduce-scatter.14.cloned.1.call-start = ((), (), s32[]{:S(2)}) async-start(), calls=%async_computation.15 | async-start | bytes 2007040 | tf_op jit(solution)/shard_map/reduce_scatter | solution.py:271
  543.9 207.0 %reduce-scatter.12.cloned.1.call-start = ((), (), s32[]{:S(2)}) async-start(), calls=%async_computation.14 | async-start | bytes 2580480 | tf_op jit(solution)/shard_map/reduce_scatter | solution.py:262
  692.4 144.0 %reduce-scatter.16.cloned.1.call-start = ((), (), s32[]{:S(2)}) async-start(), calls=%async_computation.16 | async-start | bytes 10895360 | tf_op jit(solution)/shard_map/reduce_scatter | solution.py:277
  699.8 221.9 %reduce-scatter.18.cloned.1.call-start = ((), (), s32[]{:S(2)}) async-start(), calls=%async_computation.17 | async-start | bytes 10895360 | tf_op jit(solution)/shard_map/reduce_scatter | solution.py:280
  707.1 300.0 %reduce-scatter.20.cloned.1.call-start = ((), (), s32[]{:S(2)}) async-start(), calls=%async_computation.18 | async-start | bytes 10895360 | tf_op jit(solution)/shard_map/reduce_scatter | solution.py:283
  712.8 418.0 %all-reduce.17.cloned.1.call-start = ((), (), s32[]{:S(2)}) async-start(), calls=%async_computation.21 | async-start | bytes 14909440 | tf_op jit(solution)/shard_map/psum | solution.py:289
  1009.1 6.0 copy-start.16
  1014.9 75.9 %copy-start.30 = (f32[128]{0:T(128)S(1)}, f32[128]{0:T(128)}, u32[]{:S(2)}) copy-start(f32[128]{0:T(128)} %copy-done.29) | copy-start | bytes 1540
  1130.8 4.3 copy-start.15
  1133.0 4.4 copy-start.14
  (23 other events, 49.3 us)
Sparse Core Ops, SparseCore 0:
  9.7 33.8 all-gather.7
  46.6 43.2 all-gather.9
  92.8 42.0 all-gather.11
  136.4 25.5 all-gather.13
  163.5 85.8 all-gather.15
  250.9 86.7 all-gather.17
  339.4 86.8 all-gather.19
  531.4 77.0 reduce-scatter.23
  612.4 76.9 reduce-scatter.21
  692.2 25.9 reduce-scatter.13
  721.2 29.7 reduce-scatter.11
  753.5 82.8 reduce-scatter.15
  838.8 82.8 reduce-scatter.17
  924.2 82.8 reduce-scatter.19
  1011.1 119.6 all-reduce.16
where the time goes:
time: 1160 us; the launch traced here: 1150 us
  waiting for transfers between devices  787 us (68%)
  matrix products  160 us (14%)
  blocking collectives  81.7 us (7%)
  local copies, waits for them, and re-layouts  59.3 us (5%)
  other arithmetic  40.1 us (3%)
  between operations  18.1 us (2%)
    unnamed x17, waiting for transfers between devices  147 us
    reduce_scatter x1, waiting for transfers between devices, body(): lax.psum_scatter(local_grads[6].astype(jnp.bfloat16), 'dp', scatter_dimen...  85.4 us
    reduce_scatter x1, waiting for transfers between devices, body(): lax.psum_scatter(local_grads[8].astype(jnp.bfloat16), 'dp', scatter_dimen...  85.4 us
    reduce_scatter x1, waiting for transfers between devices, body(): lax.psum_scatter(local_grads[7].astype(jnp.bfloat16), 'dp', scatter_dimen...  85.4 us
    all_gather x1, waiting for transfers between devices, body(): lax.all_gather(down_weight, 'dp', axis=0, tiled=True)  82.1 us
    all_gather x1, waiting for transfers between devices, body(): lax.all_gather(up_weight, 'dp', axis=0, tiled=True)  81.9 us
    psum x1, blocking collectives, body(): lax.psum(shard_grads[0].astype(jnp.bfloat16), 'ctx').astype(jnp.float32)  65.2 us
    all_gather x1, waiting for transfers between devices, body(): lax.all_gather(gate_weight, 'dp', axis=0, tiled=True)  49.5 us
  transfers between devices with their start and end apart: 15, of which 14 were waited for; matrix products, arithmetic and copies ran while one was open for 12% of the time, Pallas kernels for 0%

commit v1 on v0

--- a/solution.py
+++ b/solution.py
@@ -286,7 +286,9 @@
     )
     summed = (
         lax.psum(shard_grads[0].astype(jnp.bfloat16), "ctx").astype(jnp.float32),
-        lax.psum(shard_grads[1].astype(jnp.bfloat16), "ctx").astype(jnp.float32),
+        jnp.sum(lax.all_gather(shard_grads[1].astype(jnp.bfloat16), "ctx"), axis=0).astype(
+            jnp.float32
+        ),
         lax.psum(shard_grads[2].astype(jnp.bfloat16), "ctx").astype(jnp.float32),
         lax.psum(shard_grads[3].astype(jnp.bfloat16), "ctx").astype(jnp.float32),
         lax.psum(shard_grads[4].astype(jnp.bfloat16), "ctx").astype(jnp.float32),

time: 1160 us -> 1230 us (1.060)
  waiting for transfers between devices: 787 us -> 849 us
    all_gather x0 -> x1, waiting for transfers between devices: none -> 63.5 us  [body(): lax.all_gather(shard_grads[1].astype(jnp.bfloat16), 'ctx')]
    unnamed x17 -> x18, waiting for transfers between devices: 147 us -> 127 us
    reduce_scatter x1, waiting for transfers between devices: 5.32 us -> 26 us  [body(): lax.psum_scatter(local_grads[4].astype(jnp.bfloat16), 'dp', scatter_dimen...]
    unnamed x67 -> x73, local copies, waits for them, and re-layouts: 40.5 us -> 40.5 us
  transfers between devices with their start and end apart: 15 -> 16, of which waited for: 14 -> 15; matrix products, arithmetic and copies ran while one was open for 12% -> 12% of each run, Pallas kernels for 0% -> 0%
where the time goes in v1:
time: 1230 us; the launch traced here: 1220 us
  waiting for transfers between devices  849 us (69%)
  matrix products  160 us (13%)
  blocking collectives  81.4 us (7%)
  local copies, waits for them, and re-layouts  59.2 us (5%)
  other arithmetic  49.3 us (4%)
  between operations  18.2 us (1%)
    unnamed x18, waiting for transfers between devices  127 us
    reduce_scatter x1, waiting for transfers between devices, body(): lax.psum_scatter(local_grads[6].astype(jnp.bfloat16), 'dp', scatter_dimen...  86 us
    reduce_scatter x1, waiting for transfers between devices, body(): lax.psum_scatter(local_grads[7].astype(jnp.bfloat16), 'dp', scatter_dimen...  85.4 us
    reduce_scatter x1, waiting for transfers between devices, body(): lax.psum_scatter(local_grads[8].astype(jnp.bfloat16), 'dp', scatter_dimen...  85.4 us
    all_gather x1, waiting for transfers between devices, body(): lax.all_gather(down_weight, 'dp', axis=0, tiled=True)  82.1 us
    all_gather x1, waiting for transfers between devices, body(): lax.all_gather(up_weight, 'dp', axis=0, tiled=True)  82 us
    psum x1, blocking collectives, body(): lax.psum(shard_grads[0].astype(jnp.bfloat16), 'ctx').astype(jnp.float32)  64.9 us
    all_gather x1, waiting for transfers between devices, body(): lax.all_gather(shard_grads[1].astype(jnp.bfloat16), 'ctx')  63.5 us
  transfers between devices with their start and end apart: 16, of which 15 were waited for; matrix products, arithmetic and copies ran while one was open for 12% of the time, Pallas kernels for 0%

profile of v1, /device:TPU:1, one launch (start us, length us, event | category | flops | bytes accessed | tf_op | source)
XLA Modules:
  0.0 1219.5 jit_solution(7265206978152235010)
XLA Ops:
  13.2 9.4 all-reduce.14
  23.7 19.9 %all-gather.10.cloned.1.call-done = bf16[896,1152]{1,0:T(8,128)(2,1)} async-done(((bf16[224,1152]{1,0:T(8,128)(2,1)}), bf16[896,1152]{1,0:T(8,128)(2,1)}) %all-gather.10.cloned.1.call-update) | async-done | bytes 2064400 | tf_op jit(solution)/shard_map/all_gather | solution.py:82
  51.2 38.8 %all-gather.12.cloned.1.call-done = bf16[4096,128]{1,0:T(8,128)(2,1)} async-done(((bf16[128,128]{1,0:T(8,128)(2,1)}), bf16[4096,128]{1,0:T(8,128)(2,1)}) %all-gather.12.cloned.1.call-update) | async-done | bytes 1048592 | tf_op jit(solution)/shard_map/all_gather | solution.py:107
  89.9 5.0 reshape.339
  94.9 5.9 copy.88
  100.8 34.1 %all-gather.14.cloned.1.call-done = bf16[4096,128]{1,0:T(8,128)(2,1)} async-done(((bf16[128,128]{1,0:T(8,128)(2,1)}), bf16[4096,128]{1,0:T(8,128)(2,1)}) %all-gather.14.cloned.1.call-update) | async-done | bytes 1048592 | tf_op jit(solution)/shard_map/all_gather | solution.py:106
  134.9 5.0 reshape.340
  139.9 4.6 copy.89
  144.5 37.0 %while.39 = (s32[]{:T(128)}, f32[2,7,128]{2,1,0:T(8,128)S(1)}, f32[2,7,128]{2,1,0:T(8,128)S(1)}, s32[4,1024]{1,0:T(4,128)S(1)}, s32[128]{0:T(128)S(1)}, /*index=...) while((s32[]{:T(128)}, f32[2,7,128]{2,1,0:T(8,128)S(1)}, ...), condition=%wide.region_6.7_spmd.clone, body=%wide.region_3.6_spmd.clone.sunk | while | flops 247866112 | bytes 15670904 | solution.py:134
  171.7 4.7 fusion.161
  176.4 5.2 exponential_reduce_fusion.2
  181.6 15.1 %while.40 = (s32[]{:T(128)}, f32[128,2,7,64]{0,3,2,1:T(8,128)S(1)}, bf16[4,1024,2,64]{1,3,2,0:T(8,128)(2,1)}, s32[4,1024]{1,0:T(4,128)S(1)}, s32[128]{0:T(128)S(...) while((s32[]{:T(128)}, f32[128,2,7,64]{0,3,2,1:T(8,128)S(1)}, ...), condition=%wide.region_8.9_spmd.clone, body=%wide.region_7.8_spmd.clone.sunk | while | flops 477462528 | bytes 1955962 | solution.py:151
  199.9 49.5 %all-gather.18.cloned.1.call-done = bf16[896,4864]{1,0:T(8,128)(2,1)} async-done(((bf16[224,4864]{1,0:T(8,128)(2,1)}), bf16[896,4864]{1,0:T(8,128)(2,1)}) %all-gather.18.cloned.1.call-update) | async-done | bytes 8716304 | tf_op jit(solution)/shard_map/all_gather | solution.py:156
  249.3 6.4 fusion.102
  255.7 82.0 %all-gather.20.cloned.1.call-done = bf16[896,4864]{1,0:T(8,128)(2,1)} async-done(((bf16[224,4864]{1,0:T(8,128)(2,1)}), bf16[896,4864]{1,0:T(8,128)(2,1)}) %all-gather.20.cloned.1.call-update) | async-done | bytes 8716304 | tf_op jit(solution)/shard_map/all_gather | solution.py:157
  337.7 6.4 fusion.103
  344.1 82.1 %all-gather.22.cloned.1.call-done = bf16[4864,896]{1,0:T(8,128)(2,1)} async-done(((bf16[1216,896]{1,0:T(8,128)(2,1)}), bf16[4864,896]{1,0:T(8,128)(2,1)}) %all-gather.22.cloned.1.call-update) | async-done | bytes 8716304 | tf_op jit(solution)/shard_map/all_gather | solution.py:158
  426.3 7.5 multiply_convert_fusion
  433.8 7.2 fusion.104
  449.2 71.2 %while.41 = (s32[]{:T(128)}, f32[128,2,7,64]{0,3,2,1:T(8,128)S(1)}, bf16[4,1024,2,64]{1,3,2,0:T(8,128)(2,1)}, bf16[4,1024,2,64]{1,3,2,0:T(8,128)(2,1)}, bf16[4,1...) while((s32[]{:T(128)}, f32[128,2,7,64]{0,3,2,1:T(8,128)S(1)}, ...), condition=%wide.region_12.13_spmd.clone, body=%wide.region_11.12_spmd.clone.sunk | while | flops 1193361408 | bytes 99781520 | solution.py:215
  450.8 5.4 fusion.179
  460.9 5.2 fusion.182
  468.5 5.4 fusion.179
  478.7 5.2 fusion.182
  486.3 5.4 fusion.179
  496.4 5.2 fusion.182
  504.0 5.4 fusion.179
  514.2 5.2 fusion.182
  520.4 6.0 copy.124
  526.3 4.7 reshape.333
  531.2 6.0 copy.123
  537.2 4.7 reshape.331
  544.0 7.1 convolution_convert_fusion.2
  551.2 7.2 convolution_convert_fusion.1
  559.3 4.9 convolution_convert_fusion
  564.4 43.9 %reduce-scatter.24.cloned.1.call-done = bf16[128,128]{1,0:T(8,128)(2,1)} async-done(((bf16[4096,128]{1,0:T(8,128)(2,1)}), bf16[128,128]{1,0:T(8,128)(2,1)}) %reduce-scatter.24.cloned.1.call-update) | async-done | bytes 32784
  609.2 79.7 %reduce-scatter.22.cloned.1.call-done = bf16[128,128]{1,0:T(8,128)(2,1)} async-done(((bf16[4096,128]{1,0:T(8,128)(2,1)}), bf16[128,128]{1,0:T(8,128)(2,1)}) %reduce-scatter.22.cloned.1.call-update) | async-done | bytes 32784
  692.0 26.0 %reduce-scatter.14.cloned.1.call-done = bf16[224,896]{1,0:T(8,128)(2,1)} async-done(((bf16[896,896]{1,0:T(8,128)(2,1)}), bf16[224,896]{1,0:T(8,128)(2,1)}) %reduce-scatter.14.cloned.1.call-update) | async-done | bytes 401424 | tf_op jit(solution)/shard_map/reduce_scatter | solution.py:271
  718.0 86.0 %reduce-scatter.16.cloned.1.call-done = bf16[224,4864]{1,0:T(8,128)(2,1)} async-done(((bf16[896,4864]{1,0:T(8,128)(2,1)}), bf16[224,4864]{1,0:T(8,128)(2,1)}) %reduce-scatter.16.cloned.1.call-update) | async-done | bytes 2179088 | tf_op jit(solution)/shard_map/reduce_scatter | solution.py:277
  804.1 85.4 %reduce-scatter.18.cloned.1.call-done = bf16[224,4864]{1,0:T(8,128)(2,1)} async-done(((bf16[896,4864]{1,0:T(8,128)(2,1)}), bf16[224,4864]{1,0:T(8,128)(2,1)}) %reduce-scatter.18.cloned.1.call-update) | async-done | bytes 2179088 | tf_op jit(solution)/shard_map/reduce_scatter | solution.py:280
  889.5 85.4 %reduce-scatter.20.cloned.1.call-done = bf16[1216,896]{1,0:T(8,128)(2,1)} async-done(((bf16[4864,896]{1,0:T(8,128)(2,1)}), bf16[1216,896]{1,0:T(8,128)(2,1)}) %reduce-scatter.20.cloned.1.call-update) | async-done | bytes 2179088 | tf_op jit(solution)/shard_map/reduce_scatter | solution.py:283
  974.9 32.1 %reduce-scatter.12.cloned.1.call-done = bf16[224,1152]{1,0:T(8,128)(2,1)} async-done(((bf16[896,1152]{1,0:T(8,128)(2,1)}), bf16[224,1152]{1,0:T(8,128)(2,1)}) %reduce-scatter.12.cloned.1.call-update) | async-done | bytes 516112 | tf_op jit(solution)/shard_map/reduce_scatter | solution.py:262
  1009.0 5.8 fusion.65
  1015.9 7.1 all-reduce.13
  1023.2 64.9 %all-reduce.11 = (bf16[224]{0:T(256)(128)(2,1)S(1)}, bf16[256]{0:T(256)(128)(2,1)S(1)}, bf16[32]{0:T(256)(128)(2,1)S(1)}, bf16[224]{0:T(256)(128)(2,1)S(1)}) all-reduce(bf16[224]{0:T(256)(128)(2,1)S(1)} %dynamic-slice.4, bf16[256]{0:T(256)(128)(2,1)S(1)} %dynamic-slice.6, ...), channel_id=1, replica_groups=mesh['dp'=4,'ctx'=32] {'ctx'}, use_global_device_ids=true, to_apply=%region_18.19 | all-reduce | flops 736 | bytes 2944 | tf_op jit(solution)/shard_map/psum | solution.py:288
  1091.2 37.3 %all-reduce.17.cloned.1.call-done = (bf16[224,896]{1,0:T(8,128)(2,1)}, bf16[224,4864]{1,0:T(8,128)(2,1)}, bf16[224,4864]{1,0:T(8,128)(2,1)}, bf16[1216,896]{1,0:T(8,128)(2,1)}) async-done(((bf16[224,896]{1,0:T(8,128)(2,1)}, bf16[224,4864]{1,0:T(8,128)(2,1)}, bf16[224,4864]{1,0:T(8,128)(2,1)}, bf16[1216,896]{1,0:T(8,128)(2,1)}), (bf16[224,896]{1,0:T(8,128)(2,1)}, bf16[224,4864]{1,0:T(8,128)(2,1)}, ...) | async-done | bytes 6938640 | tf_op jit(solution)/shard_map/psum | solution.py:294
  1139.4 63.5 %all-gather.24.cloned.1.call-done = bf16[7168,1152]{1,0:T(8,128)(2,1)} async-done(((bf16[224,1152]{1,0:T(8,128)(2,1)}), bf16[7168,1152]{1,0:T(8,128)(2,1)}) %all-gather.24.cloned.1.call-update) | async-done | bytes 16515088 | tf_op jit(solution)/shard_map/all_gather | solution.py:289
  1202.9 8.7 reduce_sum.114
  (293 shorter events, 117.5 us)
Async XLA Ops:
  7.2 39.4 %copy-start.34 = (s32[128]{0:T(128)S(1)}, s32[128]{0:T(128)}, u32[]{:S(2)}) copy-start(s32[128]{0:T(128)} %param.21) | copy-start | bytes 1540
  7.2 36.4 %all-gather.10.cloned.1.call-start = ((), (), s32[]{:S(2)}) async-start(), calls=%async_computation.7 | async-start | bytes 2580480 | tf_op jit(solution)/shard_map/all_gather | solution.py:82
  7.9 82.0 %all-gather.12.cloned.1.call-start = ((), (), s32[]{:S(2)}) async-start(), calls=%async_computation.8 | async-start | bytes 1081344 | tf_op jit(solution)/shard_map/all_gather | solution.py:107
  22.6 24.2 %copy-start.27 = (f32[896]{0:T(1024)}, f32[896]{0:T(1024)S(1)}, u32[]{:S(2)}) copy-start(f32[896]{0:T(1024)S(1)} %convert_element_type.166) | copy-start | bytes 10756
  23.7 22.9 %copy-start.32 = (f32[128]{0:T(128)}, f32[128]{0:T(128)S(1)}, u32[]{:S(2)}) copy-start(f32[128]{0:T(128)S(1)} %fusion.73) | copy-start | bytes 1540
  23.7 22.9 %copy-start.29 = (f32[128]{0:T(128)}, f32[128]{0:T(128)S(1)}, u32[]{:S(2)}) copy-start(f32[128]{0:T(128)S(1)} %fusion.95) | copy-start | bytes 1540
  46.5 88.4 %all-gather.14.cloned.1.call-start = ((), (), s32[]{:S(2)}) async-start(), calls=%async_computation.9 | async-start | bytes 1081344 | tf_op jit(solution)/shard_map/all_gather | solution.py:106
  47.8 149.0 %all-gather.16.cloned.1.call-start = ((), (), s32[]{:S(2)}) async-start(), calls=%async_computation.10 | async-start | bytes 2007040 | tf_op jit(solution)/shard_map/all_gather | solution.py:84
  48.4 201.0 %all-gather.18.cloned.1.call-start = ((), (), s32[]{:S(2)}) async-start(), calls=%async_computation.11 | async-start | bytes 10895360 | tf_op jit(solution)/shard_map/all_gather | solution.py:156
  48.9 288.8 %all-gather.20.cloned.1.call-start = ((), (), s32[]{:S(2)}) async-start(), calls=%async_computation.12 | async-start | bytes 10895360 | tf_op jit(solution)/shard_map/all_gather | solution.py:157
  49.5 376.7 %all-gather.22.cloned.1.call-start = ((), (), s32[]{:S(2)}) async-start(), calls=%async_computation.13 | async-start | bytes 10895360 | tf_op jit(solution)/shard_map/all_gather | solution.py:158
  50.3 558.0 %reduce-scatter.24.cloned.1.call-start = ((), (), s32[]{:S(2)}) async-start(), calls=%async_computation.21 | async-start | bytes 1081344
  181.6 15.2 %copy-start.9 = (bf16[128,896]{1,0:T(8,128)(2,1)S(1)}, bf16[128,896]{1,0:T(8,128)(2,1)}, u32[]{:S(2)}) copy-start(bf16[128,896]{1,0:T(8,128)(2,1)} %param.18) | copy-start | bytes 688132
  196.7 59.0 %copy-start.18 = (f32[128,2,7,64]{0,3,2,1:T(8,128)}, f32[128,2,7,64]{0,3,2,1:T(8,128)S(1)}, u32[]{:S(2)}) copy-start(f32[128,2,7,64]{0,3,2,1:T(8,128)S(1)} %get-tuple-element.157) | copy-start | bytes 1376260
  196.8 59.0 %copy-start.16 = (bf16[128,2,7,64]{0,3,2,1:T(8,128)(2,1)}, bf16[128,2,7,64]{0,3,2,1:T(8,128)(2,1)S(1)}, u32[]{:S(2)}) copy-start(bf16[128,2,7,64]{0,3,2,1:T(8,128)(2,1)S(1)} %convert_element_type.173) | copy-start | bytes 688132
  433.8 7.2 copy-start.12
  433.8 7.2 copy-start.11
  433.8 7.2 copy-start.2
  433.8 7.2 copy-start.4
  450.5 5.7 copy-start.1
  456.2 4.7 copy-start.26
  460.9 5.3 copy-start.20
  468.3 5.7 copy-start.1
  474.0 4.7 copy-start.26
  478.6 5.3 copy-start.20
  486.0 5.7 copy-start.1
  491.7 4.7 copy-start.26
  496.4 5.3 copy-start.20
  503.8 5.7 copy-start.1
  509.5 4.7 copy-start.26
  514.1 5.3 copy-start.20
  531.1 157.8 %reduce-scatter.22.cloned.1.call-start = ((), (), s32[]{:S(2)}) async-start(), calls=%async_computation.20 | async-start | bytes 1081344
  531.1 10.9 copy-start.7
  531.1 10.9 copy-start.17
  541.9 176.1 %reduce-scatter.14.cloned.1.call-start = ((), (), s32[]{:S(2)}) async-start(), calls=%async_computation.15 | async-start | bytes 2007040 | tf_op jit(solution)/shard_map/reduce_scatter | solution.py:271
  543.8 260.3 %reduce-scatter.16.cloned.1.call-start = ((), (), s32[]{:S(2)}) async-start(), calls=%async_computation.16 | async-start | bytes 10895360 | tf_op jit(solution)/shard_map/reduce_scatter | solution.py:277
  551.2 338.3 %reduce-scatter.18.cloned.1.call-start = ((), (), s32[]{:S(2)}) async-start(), calls=%async_computation.17 | async-start | bytes 10895360 | tf_op jit(solution)/shard_map/reduce_scatter | solution.py:280
  558.4 416.4 %reduce-scatter.20.cloned.1.call-start = ((), (), s32[]{:S(2)}) async-start(), calls=%async_computation.18 | async-start | bytes 10895360 | tf_op jit(solution)/shard_map/reduce_scatter | solution.py:283
  564.2 125.6 %copy-start.28 = (f32[896]{0:T(1024)S(1)}, f32[896]{0:T(1024)}, u32[]{:S(2)}) copy-start(f32[896]{0:T(1024)} %copy-done.27) | copy-start | bytes 10756
  564.2 125.6 %copy-start.30 = (f32[128]{0:T(128)S(1)}, f32[128]{0:T(128)}, u32[]{:S(2)}) copy-start(f32[128]{0:T(128)} %copy-done.29) | copy-start | bytes 1540
  564.2 125.6 %copy-start.10 = (bf16[128,896]{1,0:T(8,128)(2,1)S(1)}, bf16[128,896]{1,0:T(8,128)(2,1)}, u32[]{:S(2)}) copy-start(bf16[128,896]{1,0:T(8,128)(2,1)} %param.18) | copy-start | bytes 688132
  564.2 442.8 %reduce-scatter.12.cloned.1.call-start = ((), (), s32[]{:S(2)}) async-start(), calls=%async_computation.14 | async-start | bytes 2580480 | tf_op jit(solution)/shard_map/reduce_scatter | solution.py:262
  692.0 436.5 %all-reduce.17.cloned.1.call-start = ((), (), s32[]{:S(2)}) async-start(), calls=%async_computation.22 | async-start | bytes 13877248 | tf_op jit(solution)/shard_map/psum | solution.py:294
  974.8 34.1 %copy-start.5 = (f32[128,896]{1,0:T(8,128)S(1)}, f32[128,896]{1,0:T(8,128)}, u32[]{:S(2)}) copy-start(f32[128,896]{1,0:T(8,128)} %copy-done.3) | copy-start | bytes 1376260
  974.9 228.1 %all-gather.24.cloned.1.call-start = ((), (), s32[]{:S(2)}) async-start(), calls=%async_computation.19 | async-start | bytes 17031168 | tf_op jit(solution)/shard_map/all_gather | solution.py:289
  1009.0 6.0 copy-start.15
  1014.7 75.6 %copy-start.33 = (f32[128]{0:T(128)S(1)}, f32[128]{0:T(128)}, u32[]{:S(2)}) copy-start(f32[128]{0:T(128)} %copy-done.32) | copy-start | bytes 1540
  1128.5 6.1 copy-start.14
  (27 other events, 69.7 us)
Sparse Core Ops, SparseCore 0:
  9.7 33.8 all-gather.9
  46.6 43.2 all-gather.11
  92.8 42.0 all-gather.13
  136.4 25.5 all-gather.15
  163.5 85.8 all-gather.17
  250.8 86.8 all-gather.19
  339.4 86.8 all-gather.21
  531.2 77.0 reduce-scatter.23
  612.2 76.6 reduce-scatter.21
  691.7 26.2 reduce-scatter.13
  720.5 83.4 reduce-scatter.15
  806.6 82.8 reduce-scatter.17
  891.9 82.8 reduce-scatter.19
  977.8 29.0 reduce-scatter.11
  1010.8 117.6 all-reduce.16
  1130.9 72.0 all-gather.23
